TPU v7x, 32 devices: a whole 2x2x4 slice. The times are simulated.
32 devices in a mesh: items: 16 (over z, y, x), au: 2 (over core).
Axes of the slice: x: 2, y: 2, z: 4, core: 2. Of those that a mesh axis runs over, the one named last changes fastest.
Arguments:
- encoder_out: bfloat16 [64, 256, 512], P('items', 'au'), may hold values from -6 to 6
- labels: int32 [64, 64], P('items', 'au'), may hold values from 1 to 1023
- lengths: int32 [64], P('items'), may hold values from 55 to 63, as said below
- starts: int32 [64, 256], P('items', 'au'), may hold values from 0 to 59, as said below
- loss_cot: float32 [64], P('items'), may hold values from -6 to 6
- embed_table: bfloat16 [1024, 512], replicated, may hold values from -6 to 6
- conv_weight: bfloat16 [2, 128, 4, 4], replicated, may hold values from -2 to 2
- conv_bias: bfloat16 [512], replicated, may hold values from -3 to 3
- norm_gain: bfloat16 [512], replicated, may hold values from 0.5 to 1.5
- norm_bias: bfloat16 [512], replicated, may hold values from -2 to 2
- dec_weight: bfloat16 [512, 512], replicated, may hold values from -0.25 to 0.25
- dec_bias: bfloat16 [512], replicated, may hold values from -2 to 2
- enc_weight: bfloat16 [512, 512], replicated, may hold values from -0.25 to 0.25
- enc_bias: bfloat16 [512], replicated, may hold values from -2 to 2
- out_weight: bfloat16 [512, 1024], replicated, may hold values from -0.75 to 0.75
- out_bias: bfloat16 [1024], replicated, may hold values from -4 to 4
Outputs:
- losses: float32 [64], P(('items', 'au'))
- enc_grad: float32 [64, 256, 512], P('items', 'au')
- table_grad: float32 [1024, 512], replicated
- conv_weight_grad: float32 [2, 128, 4, 4], replicated
- conv_bias_grad: float32 [512], replicated
- gain_grad: float32 [512], replicated
- norm_bias_grad: float32 [512], replicated
- dec_weight_grad: float32 [512, 512], replicated
- dec_bias_grad: float32 [512], replicated
- enc_weight_grad: float32 [512, 512], replicated
- enc_bias_grad: float32 [512], replicated
- out_weight_grad: float32 [512, 1024], replicated
- out_bias_grad: float32 [1024], replicated
Inputs may be any that keep to these rules, and one draw needn't show every extreme that they name: `labels`: entries at positions at or beyond an utterance's length are padding. `lengths`: the first utterance of every 4 has 63 labels. Never falling along the frames; frame 0 starts at 0; the last frame starts at the utterance's length - 4; consecutive frames differ by at most 3.
All inputs are finite; a program needn't handle non-finite values.
Results may differ from a plain program's by a relative error of at most 0.007.
Values may be sent and summed in bfloat16 or wider, within the bound.
A program may use at most 128 MiB of HBM per device.

v0:
```python
import jax
import jax.numpy as jnp
from jax import lax
from jax.sharding import PartitionSpec as P

FRAMES = 256
WINDOW = 5
VOCAB = 1024


NEGATIVE_FILL = -1e30
NORM_EPS = 1e-05


def extended(block, sides, width):
    for axis, dim in sides:
        count = lax.axis_size(axis)
        forward = [(i, i + 1) for i in range(count - 1)]
        backward = [(target, source) for source, target in forward]
        low = lax.ppermute(
            lax.slice_in_dim(block, block.shape[dim] - width, None, axis=dim), axis, forward
        )
        high = lax.ppermute(lax.slice_in_dim(block, 0, width, axis=dim), axis, backward)
        block = jnp.concatenate([low, block, high], axis=dim)
    return block


def shifted(value, axis, steps):
    count = lax.axis_size(axis)
    first, last = (max(0, -steps), min(count, count - steps))
    return lax.ppermute(value, axis, [(source, source + steps) for source in range(first, last)])


def shift_window(values, advance):
    window_len = values.shape[-1]
    padded = jnp.concatenate([values, jnp.full(values.shape, NEGATIVE_FILL, values.dtype)], axis=-1)
    picks = advance[:, None] + jnp.arange(window_len, dtype=jnp.int32)[None, :]
    return jnp.take_along_axis(padded, picks, axis=1)


def shift_back(values, retreat):
    window_len = values.shape[-1]
    padded = jnp.concatenate([jnp.full(values.shape, NEGATIVE_FILL, values.dtype), values], axis=-1)
    picks = window_len - retreat[:, None] + jnp.arange(window_len, dtype=jnp.int32)[None, :]
    return jnp.take_along_axis(padded, picks, axis=1)


def emit_forward(entry_vec, emit_lp):
    columns = [entry_vec[:, 0]]
    for column in range(1, entry_vec.shape[1]):
        columns.append(jnp.logaddexp(entry_vec[:, column], columns[-1] + emit_lp[:, column - 1]))
    return jnp.stack(columns, axis=1)


def emit_backward(onward, blank_lp, emit_lp):
    window_len = onward.shape[1]
    columns = [blank_lp[:, window_len - 1] + onward[:, window_len - 1]]
    for column in range(window_len - 2, -1, -1):
        columns.append(
            jnp.logaddexp(blank_lp[:, column] + onward[:, column], emit_lp[:, column] + columns[-1])
        )
    return jnp.stack(columns[::-1], axis=1)


def place_window(values, begin, anchor, vec_len):
    position = jnp.arange(vec_len, dtype=jnp.int32)[None, :]
    offset_at = (begin - anchor)[:, None]
    placed = jnp.full((values.shape[0], vec_len), NEGATIVE_FILL, jnp.float32)
    for column in range(values.shape[1]):
        placed = jnp.where(position == offset_at + column, values[:, column : column + 1], placed)
    return placed


def pick_window(placed, begin, anchor, window_len):
    picks = (begin - anchor)[:, None] + jnp.arange(window_len, dtype=jnp.int32)[None, :]
    return jnp.take_along_axis(placed, picks, axis=1)


def run_alpha(entry_vec, blank_tm, emit_tm, advance_tm):

    def advance_step(current, inputs):
        blank_now, emit_now, moved = inputs
        alpha_now = emit_forward(current, emit_now)
        return (shift_window(alpha_now + blank_now, moved), alpha_now)

    _, alpha_all = lax.scan(advance_step, entry_vec, (blank_tm, emit_tm, advance_tm))
    return alpha_all


def run_beta(onward_last, blank_tm, emit_tm, retreat_tm):

    def retreat_step(onward, inputs):
        blank_now, emit_now, moved = inputs
        beta_now = emit_backward(onward, blank_now, emit_now)
        return (shift_back(beta_now, moved), (beta_now, onward))

    _, (beta_all, onward_all) = lax.scan(
        retreat_step, onward_last, (blank_tm, emit_tm, retreat_tm), reverse=True
    )
    return (beta_all, onward_all)


def norm_tail(conv_out, gain_values, shift_values):
    row_mean = jnp.mean(conv_out, axis=-1, keepdims=True)
    centered = conv_out - row_mean
    row_var = jnp.mean(centered * centered, axis=-1, keepdims=True)
    normed = centered * lax.rsqrt(row_var + NORM_EPS)
    return jax.nn.silu(normed * gain_values + shift_values)


def on_device(
    encoder_out,
    labels,
    lengths,
    starts,
    loss_cot,
    embed_table,
    conv_weight,
    conv_bias,
    norm_gain,
    norm_bias,
    dec_weight,
    dec_bias,
    enc_weight,
    enc_bias,
    out_weight,
    out_bias,
):
    au_count = lax.axis_size("au")
    au_place = lax.axis_index("au")
    utt_count, frames_loc, enc_dim = encoder_out.shape
    pos_loc = labels.shape[1]
    dec_dim = embed_table.shape[1]
    joint_dim = dec_weight.shape[1]
    vocab_size = out_weight.shape[1]
    group_count = dec_dim // 4
    window_len = WINDOW
    vec_len = 2 * pos_loc + 16
    ext_rows = pos_loc + 2 * pos_loc
    first_pos = au_place * pos_loc
    lower_anchor = first_pos - pos_loc - 8
    upper_anchor = first_pos + pos_loc - pos_loc - 8
    offsets = jnp.arange(window_len, dtype=jnp.int32)
    label_ext = extended(labels, (("au", 1),), pos_loc)
    position = first_pos - 1 + jnp.arange(pos_loc + 1, dtype=jnp.int32)
    token_ids = jnp.where(
        position[None, :] == 0, 0, label_ext[:, pos_loc - 2 : pos_loc + pos_loc - 1]
    )
    valid_row = position >= 0
    embedded = jnp.take(embed_table, token_ids, axis=0)
    embedded = jnp.where(valid_row[None, :, None], embedded, jnp.zeros((), jnp.bfloat16))
    embed_prev = embedded[:, :-1].reshape(utt_count, pos_loc, group_count, 4)
    embed_cur = embedded[:, 1:].reshape(utt_count, pos_loc, group_count, 4)
    conv_out = jnp.einsum(
        "bpgi,gio->bpgo", embed_prev, conv_weight[0], preferred_element_type=jnp.float32
    )
    conv_out = conv_out + jnp.einsum(
        "bpgi,gio->bpgo", embed_cur, conv_weight[1], preferred_element_type=jnp.float32
    )
    conv_out = conv_out.reshape(utt_count, pos_loc, dec_dim) + conv_bias.astype(jnp.float32)
    hidden, tail_back = jax.vjp(
        norm_tail, conv_out, norm_gain.astype(jnp.float32), norm_bias.astype(jnp.float32)
    )
    hidden_low = hidden.astype(jnp.bfloat16)
    dec_proj = (
        jnp.einsum("bpd,dj->bpj", hidden_low, dec_weight, preferred_element_type=jnp.float32)
        + dec_bias.astype(jnp.float32)
    ).astype(jnp.bfloat16)
    dec_ext = extended(dec_proj, (("au", 1),), pos_loc)
    enc_proj = (
        jnp.einsum("btd,dj->btj", encoder_out, enc_weight, preferred_element_type=jnp.float32)
        + enc_bias.astype(jnp.float32)
    ).astype(jnp.bfloat16)
    upos = starts[:, :, None] + offsets[None, None, :]
    row_index = (upos - (first_pos - pos_loc)).reshape(utt_count, frames_loc * window_len)
    pair_labels = jnp.take_along_axis(label_ext, row_index, axis=1)
    live_pair = (upos < lengths[:, None, None]).reshape(utt_count, frames_loc * window_len)
    per_block = 1
    while (
        per_block * 2 <= utt_count
        and utt_count % (per_block * 2) == 0
        and (per_block * frames_loc * window_len < 1024)
    ):
        per_block = per_block * 2
    block_count = utt_count // per_block

    def blocked(values):
        return values.reshape((block_count, per_block) + values.shape[1:])

    def joint_values(enc_block, ext_block, row_block):
        picked = jnp.take_along_axis(ext_block, row_block[:, :, None], axis=1)
        picked = picked.reshape(per_block, frames_loc, window_len, joint_dim)
        joint_act = jnp.tanh(
            enc_block[:, :, None, :].astype(jnp.float32) + picked.astype(jnp.float32)
        )
        joint_act = joint_act.reshape(per_block * frames_loc * window_len, joint_dim)
        joint_low = joint_act.astype(jnp.bfloat16)
        logits = jnp.dot(
            joint_low, out_weight, preferred_element_type=jnp.float32
        ) + out_bias.astype(jnp.float32)
        return (joint_act, joint_low, logits)

    def forward_block(packed):
        enc_block, ext_block, row_block, label_block, live_block = packed
        _, _, logits = joint_values(enc_block, ext_block, row_block)
        log_norm = jax.nn.logsumexp(logits, axis=-1)
        blank_lp = logits[:, 0] - log_norm
        target = jnp.take_along_axis(logits, label_block.reshape(-1, 1), axis=1)[:, 0] - log_norm
        emit_lp = jnp.where(live_block.reshape(-1), target, NEGATIVE_FILL)
        return (
            blank_lp.reshape(per_block, frames_loc, window_len),
            emit_lp.reshape(per_block, frames_loc, window_len),
        )

    blank_blocks, emit_blocks = lax.map(
        forward_block,
        (
            blocked(enc_proj),
            blocked(dec_ext),
            blocked(row_index),
            blocked(pair_labels),
            blocked(live_pair),
        ),
    )
    blank_tm = jnp.swapaxes(blank_blocks.reshape(utt_count, frames_loc, window_len), 0, 1)
    emit_tm = jnp.swapaxes(emit_blocks.reshape(utt_count, frames_loc, window_len), 0, 1)
    steps_between = starts[:, 1:] - starts[:, :-1]
    zero_col = jnp.zeros((utt_count, 1), jnp.int32)
    advance_tm = jnp.swapaxes(jnp.concatenate([steps_between, zero_col], axis=1), 0, 1)
    retreat_tm = jnp.swapaxes(jnp.concatenate([zero_col, steps_between], axis=1), 0, 1)
    entry_first = jnp.broadcast_to(
        jnp.where(offsets == 0, 0.0, NEGATIVE_FILL).astype(jnp.float32), (utt_count, window_len)
    )
    terminal = jnp.broadcast_to(
        jnp.where(offsets == window_len - 1, 0.0, NEGATIVE_FILL).astype(jnp.float32),
        (utt_count, window_len),
    )
    incoming_alpha = jnp.full((utt_count, vec_len), NEGATIVE_FILL, jnp.float32)
    incoming_beta = jnp.full((utt_count, vec_len), NEGATIVE_FILL, jnp.float32)
    for section_no in range(au_count):
        entry_vec = jnp.where(
            au_place == 0,
            entry_first,
            pick_window(incoming_alpha, starts[:, 0], lower_anchor, window_len),
        )
        alpha_all = run_alpha(entry_vec, blank_tm, emit_tm, advance_tm)
        onward_last = jnp.where(
            au_place == au_count - 1,
            terminal,
            pick_window(incoming_beta, starts[:, -1], upper_anchor, window_len),
        )
        beta_all, onward_all = run_beta(onward_last, blank_tm, emit_tm, retreat_tm)
        if section_no + 1 < au_count:
            leaving_alpha = place_window(
                alpha_all[-1] + blank_tm[-1], starts[:, -1], upper_anchor, vec_len
            )
            incoming_alpha = shifted(leaving_alpha, "au", 1)
            leaving_beta = place_window(beta_all[0], starts[:, 0], lower_anchor, vec_len)
            incoming_beta = shifted(leaving_beta, "au", -1)
    log_total = jax.nn.logsumexp(alpha_all[0] + blank_tm[0] + onward_all[0], axis=-1)
    losses_local = -log_total / FRAMES
    share = utt_count // au_count
    losses_out = lax.dynamic_slice_in_dim(losses_local, au_place * share, share)
    weight_scale = -(loss_cot / FRAMES)[None, :, None]
    emit_onward = jnp.concatenate(
        [beta_all[:, :, 1:], jnp.full((frames_loc, utt_count, 1), NEGATIVE_FILL, jnp.float32)],
        axis=2,
    )
    blank_grad = weight_scale * jnp.exp(
        alpha_all + blank_tm + onward_all - log_total[None, :, None]
    )
    emit_grad = weight_scale * jnp.exp(alpha_all + emit_tm + emit_onward - log_total[None, :, None])
    blank_grad = jnp.swapaxes(blank_grad, 0, 1)
    emit_grad = jnp.swapaxes(emit_grad, 0, 1)

    def backward_block(totals, packed):
        enc_block, ext_block, row_block, label_block, blank_g, emit_g = packed
        joint_act, joint_low, logits = joint_values(enc_block, ext_block, row_block)
        log_norm = jax.nn.logsumexp(logits, axis=-1, keepdims=True)
        softmax_p = jnp.exp(logits - log_norm)
        vocab_ids = jnp.arange(vocab_size, dtype=jnp.int32)[None, :]
        blank_flat = blank_g.reshape(-1, 1)
        emit_flat = emit_g.reshape(-1, 1)
        grad_logits = (
            jnp.where(vocab_ids == 0, blank_flat, 0.0)
            + jnp.where(vocab_ids == label_block.reshape(-1, 1), emit_flat, 0.0)
            - (blank_flat + emit_flat) * softmax_p
        )
        grad_low = grad_logits.astype(jnp.bfloat16)
        out_w_total = totals[0] + jnp.einsum(
            "rj,rv->jv", joint_low, grad_low, preferred_element_type=jnp.float32
        )
        out_b_total = totals[1] + jnp.sum(grad_low.astype(jnp.float32), axis=0)
        grad_joint = jnp.einsum(
            "rv,jv->rj", grad_low, out_weight, preferred_element_type=jnp.float32
        )
        grad_pre = (grad_joint * (1.0 - joint_act * joint_act)).reshape(
            per_block, frames_loc * window_len, joint_dim
        )
        grad_enc_block = jnp.sum(
            grad_pre.reshape(per_block, frames_loc, window_len, joint_dim), axis=2
        )
        selector = (
            row_block[:, :, None] == jnp.arange(ext_rows, dtype=jnp.int32)[None, None, :]
        ).astype(jnp.bfloat16)
        upper_part = grad_pre.astype(jnp.bfloat16)
        lower_part = (grad_pre - upper_part.astype(jnp.float32)).astype(jnp.bfloat16)
        grad_ext_block = jnp.einsum(
            "bpr,bpj->brj", selector, upper_part, preferred_element_type=jnp.float32
        )
        grad_ext_block = grad_ext_block + jnp.einsum(
            "bpr,bpj->brj", selector, lower_part, preferred_element_type=jnp.float32
        )
        return ((out_w_total, out_b_total), (grad_enc_block, grad_ext_block))

    start_totals = (
        jnp.zeros((joint_dim, vocab_size), jnp.float32),
        jnp.zeros((vocab_size,), jnp.float32),
    )
    (out_w_grad, out_b_grad), (enc_proj_grad, ext_grad) = lax.scan(
        backward_block,
        start_totals,
        (
            blocked(enc_proj),
            blocked(dec_ext),
            blocked(row_index),
            blocked(pair_labels),
            blocked(blank_grad),
            blocked(emit_grad),
        ),
    )
    enc_proj_low = enc_proj_grad.reshape(utt_count, frames_loc, joint_dim).astype(jnp.bfloat16)
    enc_grad = jnp.einsum(
        "btj,dj->btd", enc_proj_low, enc_weight, preferred_element_type=jnp.float32
    )
    enc_w_grad = jnp.einsum(
        "btd,btj->dj", encoder_out, enc_proj_low, preferred_element_type=jnp.float32
    )
    enc_b_grad = jnp.sum(enc_proj_low.astype(jnp.float32), axis=(0, 1))
    ext_grad = ext_grad.reshape(utt_count, ext_rows, joint_dim)
    rim_pair = jnp.concatenate([ext_grad[:, :pos_loc], ext_grad[:, ext_rows - pos_loc :]], axis=1)
    returned = extended(rim_pair.astype(jnp.bfloat16), (("au", 1),), pos_loc).astype(rim_pair.dtype)
    dec_grad = ext_grad[:, pos_loc : pos_loc + pos_loc]
    dec_grad = dec_grad + returned[:, :pos_loc]
    dec_grad = dec_grad + returned[:, 3 * pos_loc :]
    dec_low = dec_grad.astype(jnp.bfloat16)
    dec_w_grad = jnp.einsum("bpd,bpj->dj", hidden_low, dec_low, preferred_element_type=jnp.float32)
    dec_b_grad = jnp.sum(dec_low.astype(jnp.float32), axis=(0, 1))
    hidden_grad = jnp.einsum("bpj,dj->bpd", dec_low, dec_weight, preferred_element_type=jnp.float32)
    conv_grad, gain_grad, shift_grad = tail_back(hidden_grad)
    conv_b_grad = jnp.sum(conv_grad, axis=(0, 1))
    conv_grouped = conv_grad.reshape(utt_count, pos_loc, group_count, 4)
    kernel_f = conv_weight.astype(jnp.float32)
    kernel_prev = jnp.einsum(
        "bpgi,bpgo->gio",
        embed_prev.astype(jnp.float32),
        conv_grouped,
        precision=lax.Precision.HIGHEST,
    )
    kernel_cur = jnp.einsum(
        "bpgi,bpgo->gio",
        embed_cur.astype(jnp.float32),
        conv_grouped,
        precision=lax.Precision.HIGHEST,
    )
    conv_w_grad = jnp.stack([kernel_prev, kernel_cur])
    embed_prev_grad = jnp.einsum(
        "bpgo,gio->bpgi", conv_grouped, kernel_f[0], precision=lax.Precision.HIGHEST
    ).reshape(utt_count, pos_loc, dec_dim)
    embed_cur_grad = jnp.einsum(
        "bpgo,gio->bpgi", conv_grouped, kernel_f[1], precision=lax.Precision.HIGHEST
    ).reshape(utt_count, pos_loc, dec_dim)
    embed_grad = jnp.pad(embed_prev_grad, ((0, 0), (0, 1), (0, 0))) + jnp.pad(
        embed_cur_grad, ((0, 0), (1, 0), (0, 0))
    )
    embed_grad = jnp.where(valid_row[None, :, None], embed_grad, 0.0)
    table_grad = jax.ops.segment_sum(
        embed_grad.reshape(-1, dec_dim), token_ids.reshape(-1), num_segments=VOCAB
    )
    grad_set = (
        table_grad,
        conv_w_grad,
        conv_b_grad,
        gain_grad,
        shift_grad,
        dec_w_grad,
        dec_b_grad,
        enc_w_grad,
        enc_b_grad,
        out_w_grad,
        out_b_grad,
    )
    summed = lax.psum(
        (
            grad_set[0],
            grad_set[1],
            grad_set[2],
            grad_set[3],
            grad_set[4],
            grad_set[5],
            grad_set[6],
            grad_set[7],
            grad_set[8],
            grad_set[9],
            grad_set[10],
        ),
        ("items", "au"),
    )
    return (
        losses_out,
        enc_grad,
        summed[0],
        summed[1],
        summed[2],
        summed[3],
        summed[4],
        summed[5],
        summed[6],
        summed[7],
        summed[8],
        summed[9],
        summed[10],
    )


def solution(mesh):
    in_specs = (
        P("items", "au", None),
        P("items", "au"),
        P("items"),
        P("items", "au"),
        P("items"),
        P(),
        P(),
        P(),
        P(),
        P(),
        P(),
        P(),
        P(),
        P(),
        P(),
        P(),
    )
    out_specs = (
        P(("items", "au")),
        P("items", "au", None),
        P(),
        P(),
        P(),
        P(),
        P(),
        P(),
        P(),
        P(),
        P(),
        P(),
        P(),
    )
    return jax.shard_map(
        on_device, mesh=mesh, in_specs=in_specs, out_specs=out_specs, check_vma=False
    )
```

profile of v0, /device:TPU:1, one launch (start us, length us, event | category | flops | bytes accessed | tf_op | source)
XLA Modules:
  0.0 1592.1 jit_solution(4724605460348074676)
XLA Ops:
  8.7 3.0 collective-permute-start.3
  31.8 21.1 %gather_fusion.8 = s32[2560]{0:T(1024)S(1)} fusion(s32[4,96]{1,0:T(4,128)S(1)} %pad_add_fusion.1, s32[2560]{0:T(1024)S(1)} %reshape.695), kind=kCustom, calls=%fused_computation.12 | custom fusion | bytes 40960 | tf_op jit(solution)/shard_map/jit(take_along_axis)/gather | solution.py:176
  53.1 104.8 %while.87 = (s32[]{:T(128)}, f32[2,2,128,5]{3,1,0,2:T(2,128)S(1)}, f32[2,2,128,5]{3,1,0,2:T(2,128)}, bf16[2,2,128,512]{3,2,1,0:T(8,128)(2,1)S(1)}, bf16[2,2,96,5...) while((s32[]{:T(128)}, f32[2,2,128,5]{3,1,0,2:T(2,128)S(1)}, ...), condition=%wide.region_5.8_spmd, body=%wide.region_2.0_spmd.sunk | while | flops 1350222336 | bytes 41650148 | solution.py:215
  53.5 2.5 add.2014
  56.0 4.6 add.2015
  60.6 8.8 gather_fusion
  71.1 5.2 fusion.136
  76.4 22.7 %gather_fusion.1 = f32[1280]{0:T(1024)S(1)} fusion(f32[1280,1024]{0,1:T(8,128)} %get-tuple-element.1120, s32[1280]{0:T(1024)S(1)} %fusion.137), kind=kCustom, calls=%fused_computation.2.clone.1 | custom fusion | bytes 20480 | tf_op jit(solution)/shard_map/while/body/eval_jaxpr/jit(take_along_axis)/gather | solution.py:208
  99.6 3.3 exponential_reduce_fusion.4
  105.7 2.5 add.2014
  108.2 4.6 add.2015
  112.9 8.8 gather_fusion
  123.4 5.2 fusion.136
  128.7 23.0 %gather_fusion.1 = f32[1280]{0:T(1024)S(1)} fusion(f32[1280,1024]{0,1:T(8,128)} %get-tuple-element.1120, s32[1280]{0:T(1024)S(1)} %fusion.137), kind=kCustom, calls=%fused_computation.2.clone.1 | custom fusion | bytes 20480 | tf_op jit(solution)/shard_map/while/body/eval_jaxpr/jit(take_along_axis)/gather | solution.py:208
  152.1 3.3 exponential_reduce_fusion.4
  158.0 373.7 %while.90 = (s32[]{:T(128)}, f32[4,5]{1,0:T(4,128)S(1)}, f32[128,4,5]{2,1,0:T(4,128)S(1)}, f32[128,4,5]{2,1,0:T(4,128)S(1)}, f32[128,4,5]{2,1,0:T(4,128)}, /*ind...) while((s32[]{:T(128)}, f32[4,5]{1,0:T(4,128)S(1)}, f32[128,4,5]{2,1,0:T(4,128)S(1)}, ...), condition=%wide.region_11.15_spmd, body=%wide.region_10.14_spmd.sunk | while | flops 511 | bytes 6353 | solution.py:97
  532.1 2.9 collective-permute-start.5
  535.1 274.1 %while.88 = (s32[]{:T(128)}, f32[4,5]{1,0:T(4,128)S(1)}, f32[128,4,5]{2,1,0:T(4,128)S(1)}, f32[128,4,5]{2,1,0:T(4,128)}, f32[128,4,5]{2,1,0:T(4,128)S(1)}, /*index=5*/s32[128,4]{1,0:T(8,128)S(1)}, s32[]{:T(128)}, f32[]{:T(128)}) while((s32[]{:T(128)}, f32[4,5]{1,0:T(4,128)S(1)}, f32[128,4,5]{2,1,0:T(4,128)S(1)}, f32[128,4,5]{2,1,0:T(4,128)}, ...), condition=%wide.region_7.11_spmd, body=%wide.region_6.10_spmd.sunk | while | flops 506 | bytes 6177 | solution.py:86
  813.7 286.8 %while.91 = (s32[]{:T(128)}, f32[4,5]{1,0:T(4,128)S(1)}, f32[128,4,5]{2,1,0:T(4,128)S(1)}, f32[128,4,5]{2,1,0:T(4,128)S(1)}, f32[128,4,5]{2,1,0:T(4,128)S(1)}, /...) while((s32[]{:T(128)}, f32[4,5]{1,0:T(4,128)S(1)}, ...), condition=%wide.region_13.17_spmd, body=%wide.region_12.16_spmd.sunk | while | flops 511 | bytes 10461 | solution.py:97
  1100.6 187.0 %while.89 = (s32[]{:T(128)}, f32[4,5]{1,0:T(4,128)S(1)}, f32[128,4,5]{2,1,0:T(4,128)S(1)}, f32[128,4,5]{2,1,0:T(4,128)S(1)}, f32[128,4,5]{2,1,0:T(4,128)S(1)}, /*index=5*/s32[128,4]{1,0:T(8,128)S(1)}, s32[]{:T(128)}, f32[]{:T(128)}) while((s32[]{:T(128)}, f32[4,5]{1,0:T(4,128)S(1)}, f32[128,4,5]{2,1,0:T(4,128)S(1)}, ...), condition=%wide.region_9.13_spmd, body=%wide.region_8.12_spmd.sunk | while | flops 506 | bytes 6177 | solution.py:86
  1289.7 106.8 %while.92 = (s32[]{:T(128)}, f32[512,1024]{1,0:T(8,128)}, f32[1024]{0:T(1024)S(1)}, bf16[2,2,128,512]{3,2,1,0:T(8,128)(2,1)S(1)}, f32[2,2,96,512]{3,2,1,0:T(8,12...) while((s32[]{:T(128)}, f32[512,1024]{1,0:T(8,128)}, ...), condition=%wide.region_21.25_spmd.clone, body=%wide.region_16.24_spmd.clone.sunk | while | flops 4307790848 | bytes 157358128 | solution.py:320
  1290.0 2.5 add.2079
  1292.5 4.5 add.2080
  1297.1 12.1 gather_fusion.6
  1317.2 5.1 convert_reduce_fusion.4
  1322.3 5.2 select_add_fusion.4
  1327.5 3.4 convolution_multiply_fusion.2
  1330.9 4.3 reshape.895
  1335.3 3.5 reduce_sum.175
  1338.9 2.3 fusion.155
  1342.8 2.5 add.2079
  1345.3 4.5 add.2080
  1349.9 12.1 gather_fusion.6
  1370.0 5.1 convert_reduce_fusion.4
  1375.2 5.8 select_add_fusion.4
  1381.0 3.4 convolution_multiply_fusion.2
  1384.4 4.3 reshape.895
  1388.8 3.5 reduce_sum.175
  1392.4 2.2 fusion.155
  1397.9 3.0 collective-permute-start.7
  1402.2 2.5 convolution_bitcast_fusion
  1408.2 2.2 convolution_bitcast_fusion.3
  1414.3 2.9 scatter_custom_fusion
  1420.0 2.0 convolution_bitcast_fusion.4
  1422.1 2.0 convolution_bitcast_fusion.5
  1424.2 43.3 %all-reduce.7 = (f32[2,128,4,4]{1,3,2,0:T(4,128)}, f32[512]{0:T(512)}, f32[512]{0:T(512)}, f32[512]{0:T(512)}, f32[512]{0:T(512)}, /*index=5*/f32[512]{0:T(512)}, f32[1024]{0:T(1024)}) all-reduce(f32[2,128,4,4]{1,3,2,0:T(4,128)S(1)} %pad_maximum_fusion.4, ...), channel_id=1, replica_groups=mesh['items'=16,'au'=2] {'items','au'}, use_global_device_ids=true, to_apply=%region_26.30 | all-reduce | flops 7680 | bytes 61440 | tf_op jit(solution)/shard_map/psum | solution.py:393
  1467.6 110.3 %all-reduce.11.cloned.1.call-done = (f32[1024,512]{1,0:T(8,128)}, f32[512,512]{1,0:T(8,128)}, f32[512,512]{0,1:T(8,128)}, f32[512,1024]{1,0:T(8,128)}) async-done(((f32[1024,512]{1,0:T(8,128)}, f32[512,512]{1,0:T(8,128)}, f32[512,512]{0,1:T(8,128)}, f32[512,1024]{1,0:T(8,128)}), (f32[1024,512]{1,0:T(8,128)}, f32[512,512]{1,0:T(8,128)}, f32[512,512]{0,1:T(8,128)}, ...) | async-done | bytes 6291472 | tf_op jit(solution)/shard_map/psum | solution.py:393
  1577.9 2.7 copy.135
  (6675 shorter events, 1186.3 us)
Async XLA Ops:
  7.2 14.8 copy-start
  7.2 10.9 copy-start.60
  7.2 10.9 copy-start.61
  7.2 10.9 copy-start.45
  7.2 11.4 copy-start.68
  7.2 1570.7 %all-reduce.11.cloned.1.call-start = ((), (), s32[]{:S(2)}) async-start(), calls=%async_computation | async-start | bytes 12582912 | tf_op jit(solution)/shard_map/psum | solution.py:393
  7.3 14.4 collective-permute-start
  8.7 23.0 %collective-permute-start.3 = (s32[4,32]{1,0:T(4,128)}, s32[4,32]{1,0:T(4,128)S(1)}, u32[]{:S(2)}, u32[]{:S(2)}) collective-permute-start(s32[4,32]{1,0:T(4,128)} %param.35), channel_id=1, source_target_pairs={{1,0},{3,2},{5,4},{7,6},{9,8},{11,10},{13,12},{15,14},{17,16},{19,... | collective-permute-start | bytes 1544 | tf_op jit(solution)/shard_map/ppermute | solution.py:23
  11.8 8.2 copy-start.56
  11.8 11.1 copy-start.47
  13.3 14.2 copy-start.37
  14.1 5.9 copy-start.25
  14.1 5.9 copy-start.26
  15.4 5.1 copy-start.58
  18.4 6.0 copy-start.19
  20.8 6.7 copy-start.54
  20.8 6.7 copy-start.39
  27.0 26.0 %copy-start.11 = (f32[4,32,512]{2,1,0:T(8,128)}, f32[4,32,512]{2,1,0:T(8,128)S(1)}, u32[]{:S(2)}) copy-start(f32[4,32,512]{2,1,0:T(8,128)S(1)} %copy.112) | copy-start | bytes 786436
  28.9 24.1 %collective-permute-start.2 = (bf16[4,32,512]{2,1,0:T(8,128)(2,1)S(1)}, bf16[4,32,512]{2,1,0:T(8,128)(2,1)S(1)}, u32[]{:S(2)}, u32[]{:S(2)}) collective-permute-start(bf16[4,32,512]{2,1,0:T(8,128)(2,1)S(1)} %fusion.44), channel_id=1, source_target_pairs={{1,0},{3,2},{5,4},{7,6},{9,8},{11,10},{13,12},{15,14},{17,16},{19,... | collective-permute-start | bytes 393224 | tf_op jit(solution)/shard_map/ppermute | solution.py:23
  30.2 22.8 %collective-permute-start.1 = (bf16[4,32,512]{2,1,0:T(8,128)(2,1)S(1)}, bf16[4,32,512]{2,1,0:T(8,128)(2,1)S(1)}, u32[]{:S(2)}, u32[]{:S(2)}) collective-permute-start(bf16[4,32,512]{2,1,0:T(8,128)(2,1)S(1)} %fusion.44), channel_id=1, source_target_pairs={{0,1},{2,3},{4,5},{6,7},{8,9},{10,11},{12,13},{14,15},{16,17},{18,... | collective-permute-start | bytes 393224 | tf_op jit(solution)/shard_map/ppermute | solution.py:20
  31.8 21.3 %copy-start.28 = (f32[2,2,128,5]{3,1,0,2:T(2,128)S(1)}, f32[2,2,128,5]{3,1,0,2:T(2,128)}, u32[]{:S(2)}) copy-start(f32[2,2,128,5]{3,1,0,2:T(2,128)} %custom-call.38) | copy-start | bytes 30724
  31.8 21.3 %copy-start.34 = (bf16[1024]{0:T(1024)(128)(2,1)S(1)}, bf16[1024]{0:T(1024)(128)(2,1)}, u32[]{:S(2)}) copy-start(bf16[1024]{0:T(1024)(128)(2,1)} %param.49) | copy-start | bytes 6148
  99.6 4.8 copy-start.31
  152.1 4.8 copy-start.31
  158.0 374.0 %copy-start.50 = (s32[4]{0:T(128)S(1)}, s32[4]{0:T(128)}, u32[]{:S(2)}) copy-start(s32[4]{0:T(128)} %get-tuple-element.641) | copy-start | bytes 52
  158.0 374.0 %copy-start.51 = (s32[4]{0:T(128)S(1)}, s32[4]{0:T(128)}, u32[]{:S(2)}) copy-start(s32[4]{0:T(128)} %get-tuple-element.642) | copy-start | bytes 52
  158.0 374.0 %copy-start.52 = (s32[4]{0:T(128)S(1)}, s32[4]{0:T(128)}, u32[]{:S(2)}) copy-start(s32[4]{0:T(128)} %get-tuple-element.643) | copy-start | bytes 52
  158.0 374.0 %copy-start.53 = (s32[4]{0:T(128)S(1)}, s32[4]{0:T(128)}, u32[]{:S(2)}) copy-start(s32[4]{0:T(128)} %get-tuple-element.644) | copy-start | bytes 52
  532.1 279.4 %collective-permute-start.5 = (f32[4,80]{1,0:T(4,128)S(1)}, f32[4,80]{1,0:T(4,128)S(1)}, u32[]{:S(2)}, u32[]{:S(2)}) collective-permute-start(f32[4,80]{1,0:T(4,128)S(1)} %select_select_fusion.5), channel_id=1, source_target_pairs={{1,0},{3,2},{5,4},{7,6},{9,8},{11,10},{13,12},{15,14},{17,16},{19,... | collective-permute-start | bytes 3848 | tf_op jit(solution)/shard_map/ppermute | solution.py:31
  535.0 274.4 %copy-start.49 = (s32[4]{0:T(128)S(1)}, s32[4]{0:T(128)}, u32[]{:S(2)}) copy-start(s32[4]{0:T(128)} %get-tuple-element.648) | copy-start | bytes 52
  535.1 275.8 %copy-start.69 = (f32[4]{0:T(128)S(1)}, f32[4]{0:T(128)}, u32[]{:S(2)}) copy-start(f32[4]{0:T(128)} %param.38) | copy-start | bytes 52
  809.5 3.0 collective-permute-start.4
  1322.3 5.2 copy-start.5
  1322.3 5.2 copy-start.6
  1322.3 5.2 copy-start.66
  1375.2 5.8 copy-start.5
  1375.2 5.8 copy-start.6
  1375.2 5.8 copy-start.66
  1396.5 9.2 copy-start.12
  1396.5 9.2 copy-start.36
  1396.5 9.2 copy-start.38
  1396.5 9.2 copy-start.40
  1396.5 9.2 copy-start.42
  1396.5 9.2 copy-start.55
  1396.6 9.2 copy-start.67
  1397.9 6.8 collective-permute-start.7
  1400.8 3.8 collective-permute-start.6
  1417.2 4.9 copy-start.14
  (46 other events, 113.5 us)
Sparse Core Ops, SparseCore 0:
  1417.3 160.5 all-reduce.10
where the time goes:
time: 1610 us; the launch traced here: 1590 us
  local copies, waits for them, and re-layouts  967 us (60%)
  other arithmetic  375 us (23%)
  waiting for transfers between devices  110 us (7%)
  matrix products  53.8 us (3%)
  blocking collectives  43.3 us (3%)
    gather x768, local copies, waits for them, and re-layouts, shift_window(): return jnp.take_along_axis(padded, picks, axis=1)  260 us
    gather x768, local copies, waits for them, and re-layouts, shift_back(): return jnp.take_along_axis(padded, picks, axis=1)  259 us
    sub x256, other arithmetic, shift_back(): window_len - retreat[:, None]  179 us
    squeeze x640, local copies, waits for them, and re-layouts, run_alpha(): lax.scan(advance_step, entry_vec, (blank_tm, emit_tm, advance_tm))  177 us
    psum x1, waiting for transfers between devices, on_device(): lax.psum((grad_set[0], grad_set[1], grad_set[2], grad_set[3], grad_set[4]...  110 us
    gather x4, local copies, waits for them, and re-layouts, forward_block(): jnp.take_along_axis(logits, label_block.reshape(-1, 1), axis=1)[:, 0]  46.1 us
    psum x1, blocking collectives, on_device(): lax.psum((grad_set[0], grad_set[1], grad_set[2], grad_set[3], grad_set[4]...  43.3 us
    gather x8, local copies, waits for them, and re-layouts, joint_values(): picked = jnp.take_along_axis(ext_block, row_block[:, :, None], axis=1)  41.8 us

commit v1 on v0

v1 whole, which is shorter than its diff:
```python
import functools

import jax
import jax.numpy as jnp
from jax import lax
from jax.experimental import pallas as pl
from jax.experimental.pallas import tpu as pltpu
from jax.sharding import PartitionSpec as P

WINDOW = 5
NEGATIVE_FILL = -1e30
NORM_EPS = 1e-05
F32 = jnp.float32
BF16 = jnp.bfloat16
MIB = 1 << 20
MESH = pl.DeviceIdType.MESH


def dot(a, b):
    return lax.dot_general(a, b, (((1,), (0,)), ((), ())), preferred_element_type=F32)


def dot_nt(a, b):
    return lax.dot_general(a, b, (((1,), (1,)), ((), ())), preferred_element_type=F32)


def halves(x):
    high = x.astype(BF16)
    return high, (x - high.astype(F32)).astype(BF16)


def iota(shape, dim):
    return lax.broadcasted_iota(jnp.int32, shape, dim)


def column_of(row):
    return jnp.transpose(jnp.broadcast_to(row, (128, row.shape[1])))


def shift_rows(x, moved):
    out = x
    for step in (1, 2, 3):
        out = jnp.where(moved == step, pltpu.roll(x, step, 0), out)
    return out


def lattice(blank, emit, moved, scale, frames):
    lanes = blank.shape[1]
    row = iota((8, lanes), 0)
    lane = iota((8, lanes), 1) % frames
    window_row = row < WINDOW
    before = jnp.where(
        lane == 0, jnp.where(row == 0, 0.0, NEGATIVE_FILL), pltpu.roll(blank, 1, 1)
    )
    path = jnp.where(row == 0, 0.0, NEGATIVE_FILL)
    prefix = []
    for k in range(WINDOW):
        if k:
            path = jnp.where(
                row == k, 0.0, jnp.where(row < k, path + emit[k - 1 : k], NEGATIVE_FILL)
            )
        prefix.append(shift_rows(path, moved) + before)
    reach = 1
    while reach < frames:
        earlier = [pltpu.roll(column, reach, 1) for column in prefix]
        joined = []
        for k in range(WINDOW):
            terms = [earlier[i] + prefix[k][i : i + 1] for i in range(WINDOW)]
            top = functools.reduce(jnp.maximum, terms)
            total = functools.reduce(jnp.add, [jnp.exp(term - top) for term in terms])
            joined.append(top + jnp.log(total))
        prefix = [jnp.where(lane >= reach, new, old) for new, old in zip(joined, prefix)]
        reach *= 2
    alpha = jnp.concatenate(
        [column[:1] for column in prefix] + [jnp.full((8 - WINDOW, lanes), NEGATIVE_FILL, F32)], axis=0
    )
    leaving = alpha + blank
    arrived = pltpu.roll(leaving, 1, 1)
    entry = arrived
    for step in (1, 2, 3):
        entry = jnp.where(moved == step, pltpu.roll(arrived, 8 - step, 0), entry)
    entry = jnp.where(lane == 0, jnp.where(row == 0, 0.0, NEGATIVE_FILL), entry)
    lead = pltpu.roll(alpha + emit, 1, 0) - entry
    from_emit = jnp.where(window_row & (row > 0), 1.0 / (1.0 + jnp.exp(-lead)), 0.0)
    from_entry = jnp.where(row == 0, 1.0, jnp.where(window_row, 1.0 / (1.0 + jnp.exp(lead)), 0.0))
    suffix = []
    flow = jnp.zeros((8, lanes), F32)
    for n in range(WINDOW):
        flow = jnp.where(row == n, from_entry, flow * from_emit[n : n + 1])
        suffix.append(jnp.where(window_row, shift_rows(flow, moved), 0.0))
    reach = 1
    while reach < frames:
        later = [pltpu.roll(column, lanes - reach, 1) for column in suffix]
        joined = []
        for n in range(WINDOW):
            terms = [suffix[i] * later[n][i : i + 1] for i in range(WINDOW)]
            joined.append(functools.reduce(jnp.add, terms))
        suffix = [
            jnp.where(lane < frames - reach, new, old) for new, old in zip(joined, suffix)
        ]
        reach *= 2
    outward = jnp.where(
        lane == frames - 1,
        jnp.where(row == WINDOW - 1, 1.0, 0.0),
        pltpu.roll(suffix[WINDOW - 1], lanes - 1, 1),
    )
    state = jnp.zeros((1, lanes), F32)
    upward = [None] * WINDOW
    for k in range(WINDOW - 1, -1, -1):
        upward[k] = state
        state = outward[k : k + 1] + state
        if k:
            state = state * from_emit[k : k + 1]
    emitted = jnp.concatenate(upward + [jnp.zeros((8 - WINDOW, lanes), F32)], axis=0)
    return leaving, outward * scale, emitted * scale


BLOCKS = 6
UNITS = BLOCKS // 2
LEVELS = 32000.0

WHOLE = 12582912.0


def coded(value):
    top = jnp.maximum(jnp.max(jnp.abs(value), axis=0, keepdims=True), 1e-30)
    code = (value * (LEVELS / top) + WHOLE) - WHOLE
    return code.astype(jnp.int32).astype(jnp.int16), top * (1.0 / LEVELS)


def decoded(code, scale):
    return code.astype(jnp.int32).astype(F32) * scale


def wide(row, count):
    return jnp.concatenate([row] * count, axis=1)


def main_kernel(
    share,
    rounds,
    lengths_ref,
    cot_ref,
    labels_own_ref,
    starts_own_ref,
    conv_w_ref,
    conv_b_ref,
    gain_ref,
    shift_ref,
    dec_b_ref,
    enc_b_ref,
    out_b_ref,
    enc_hbm,
    table_hbm,
    dec_w_hbm,
    enc_w_hbm,
    out_w_hbm,
    loss_ref,
    enc_g_own_hbm,
    enc_g_far_hbm,
    small_total_ref,
    total_hbm,
    labels_far_ref,
    starts_far_ref,
    enc_own_ref,
    enc_far_ref,
    table_ref,
    dec_w_ref,
    enc_w_ref,
    out_w_ref,
    out_wt_ref,
    bias_ref,
    dec_t_ref,
    enc_t_ref,
    raw_a_ref,
    raw_b_ref,
    exp_ref,
    act_ref,
    low_ref,
    glow_ref,
    blank_ref,
    emit_ref,
    inv_ref,
    wide_label_ref,
    blank_g_ref,
    emit_g_ref,
    factor_ref,
    enc_sum_ref,
    dec_sum_ref,
    starts_ref,
    grads_ref,
    small_ref,
    enc_g_send_ref,
    enc_g_own_ref,
    total_ref,
    send_core,
    send_one,
    send_two,
    take_core,
    take_one,
    take_two,
    send_line,
    take_line,
    send_scale,
    take_scale,
    small_now,
    small_take,
    far_now,
    far_take,
    load_sems,
    swap_sems,
    code_sems,
    scale_sems,
    gather_sems,
    sent_sems,
    small_sems,
    far_sems,
    enc_sems,
    out_sems,
):
    core = lax.axis_index("au")
    item = lax.axis_index("items")
    utts = share
    half = starts_own_ref.shape[1]
    positions = 2 * labels_own_ref.shape[1]
    frames = 2 * half
    width, vocab = out_w_ref.shape
    rows = utts * positions
    lanes = utts * frames
    chunks = utts * WINDOW
    first = core * share

    loads = []
    for at, (source, target) in enumerate(
        (
            (enc_w_hbm, enc_w_ref),
            (enc_hbm.at[pl.ds(first, share)], enc_own_ref),
            (out_w_hbm, out_w_ref),
            (table_hbm, table_ref),
            (dec_w_hbm, dec_w_ref),
        )
    ):
        loads.append(pltpu.make_async_copy(source, target, load_sems.at[at]))
        loads[-1].start()
    load_enc_w, load_enc, load_out_w, load_table, load_dec_w = loads

    bit_x = item % 2
    bit_y = (item // 2) % 2
    line = (item // 4) % 4
    base = item - line * 4
    other = {"items": item, "au": 1 - core}
    to_x = {"items": item + 1 - 2 * bit_x, "au": core}
    to_y = {"items": item + 2 - 4 * bit_y, "au": core}
    peers = []
    for step in (1, 2, 3):
        low = line % 2
        high = line // 2
        low = 1 - low if step % 2 else low
        high = 1 - high if step // 2 else high
        peers.append((low + 2 * high, {"items": base + 4 * (low + 2 * high), "au": core}))
    far = []
    for r in range(rounds):
        bit = (item // (16 << r)) % 2
        far.append({"items": item + (16 << r) * (1 - 2 * bit), "au": core})
    everyone = [other, to_x, to_y] + [peer for _, peer in peers] + far

    barrier = pltpu.get_barrier_semaphore()
    for device in everyone:
        pl.semaphore_signal(barrier, inc=1, device_id=device, device_id_type=MESH)
    pl.semaphore_wait(barrier, len(everyone))

    pending = []

    def send(source, target, sems, device):
        copy = pltpu.make_async_remote_copy(
            src_ref=source,
            dst_ref=target,
            send_sem=sems.at[0],
            recv_sem=sems.at[1],
            device_id=device,
            device_id_type=MESH,
        )
        copy.start()
        pending.append(copy)
        return copy

    def push(source, target, sent, landed, device):
        pltpu.make_async_remote_copy(
            src_ref=source,
            dst_ref=target,
            send_sem=sent,
            recv_sem=landed,
            device_id=device,
            device_id_type=MESH,
        ).start()

    def settled(ref, sem):
        pltpu.make_async_copy(ref, ref, sem).wait()

    swap_labels = send(labels_own_ref, labels_far_ref, swap_sems.at[0], other)
    swap_starts = send(starts_own_ref, starts_far_ref, swap_sems.at[1], other)
    swap_enc = send(
        enc_hbm.at[pl.ds((1 - core) * share, share)], enc_far_ref, swap_sems.at[2], other
    )

    flights = {}
    depth = grads_ref.shape[4]
    piece = depth // 4

    def on_line(place):
        return pl.ds(pl.multiple_of(place * piece, piece), piece)

    def pack(value, code_ref, scale_ref):
        value = value.reshape(-1, width)
        code, scale = coded(value)
        code_ref[...] = code.reshape(code_ref.shape)
        scale_ref[...] = scale

    def unpack(code_ref, scale_ref):
        return decoded(code_ref[...], scale_ref[...])

    def ship(u, slot, source, target, scale_at, device):
        push(source, target, sent_sems.at[u, 0], code_sems.at[u, slot], device)
        push(
            send_scale.at[(u,) + scale_at],
            take_scale.at[(u,) + scale_at],
            sent_sems.at[u, 1],
            scale_sems.at[u, slot],
            device,
        )

    def landed(u, slot, target, scale_at):
        settled(target, code_sems.at[u, slot])
        settled(take_scale.at[(u,) + scale_at], scale_sems.at[u, slot])

    def held(j, u):
        return grads_ref.at[2 * u + j, core]

    def stage0(u):
        for j in range(2):
            pack(grads_ref[2 * u + j, 1 - core], send_core.at[u, j], send_scale.at[u, 0, j])
        ship(u, 0, send_core.at[u], take_core.at[u], (0,), other)

    def stage1(u):
        ways = (
            (0, (1 - bit_x,), (bit_x,), to_x),
            (1, (slice(None), 1 - bit_y), (slice(None), bit_y), to_y),
        )
        landed(u, 0, take_core.at[u], (0,))

        def part(j, at):
            return held(j, u)[at] + decoded(take_core[(u, j) + at], take_scale[u, 0, j])

        for j, away, _, _ in ways:
            pack(part(j, away), send_one.at[u, j], send_scale.at[u, 1, j])
        for j, _, _, device in ways:
            ship(u, 1 + j, send_one.at[u, j], take_one.at[u, j], (1, j), device)
        for j, _, keep, _ in ways:
            held(j, u)[keep] = part(j, keep)

    def stage2(u):
        ways = (
            (0, (bit_x, 1 - bit_y), bit_y, to_y),
            (1, (1 - bit_x, bit_y), bit_x, to_x),
        )
        for j in range(2):
            landed(u, 1 + j, take_one.at[u, j], (1, j))
        for j, away, here, _ in ways:
            value = decoded(take_one[u, j, 1 - here], take_scale[u, 1, j])
            pack(held(j, u)[away] + value, send_two.at[u, j], send_scale.at[u, 2, j])
        for j, _, _, device in ways:
            ship(u, 3 + j, send_two.at[u, j], take_two.at[u, j], (2, j), device)
        for j, _, here, _ in ways:
            held(j, u)[bit_x, bit_y] += decoded(take_one[u, j, here], take_scale[u, 1, j])

    def stage3(u):
        for j in range(2):
            landed(u, 3 + j, take_two.at[u, j], (2, j))
        for j in range(2):
            value = held(j, u)[bit_x, bit_y] + unpack(take_two.at[u, j], take_scale.at[u, 2, j])
            pack(value, send_line.at[u, j], send_scale.at[u, 3, j])
            held(j, u)[bit_x, bit_y] = value
        for step, (place, device) in enumerate(peers):
            push(
                send_line.at[u, :, on_line(place), :],
                take_line.at[u, step],
                sent_sems.at[u, 0],
                code_sems.at[u, 5],
                device,
            )
            push(
                send_scale.at[u, 3],
                take_scale.at[u, 3 + step],
                sent_sems.at[u, 1],
                scale_sems.at[u, 5],
                device,
            )

    def stage4(u):
        landed(u, 5, take_line.at[u], (pl.ds(3, 3),))
        for j in range(2):
            value = held(j, u)[bit_x, bit_y, on_line(line), :]
            for step in range(3):
                value = value + unpack(take_line.at[u, step, j], take_scale.at[u, 3 + step, j])
            for r in range(rounds):
                far_now[r, 2 * u + j] = value
                send(
                    far_now.at[r, 2 * u + j],
                    far_take.at[r, 2 * u + j],
                    far_sems.at[r, 2 * u + j],
                    far[r],
                ).wait_recv()
                value = value + far_take[r, 2 * u + j]
            total_ref[2 * u + j, core, bit_x, bit_y, on_line(line), :] = value.astype(BF16)
        place = total_ref.at[pl.ds(2 * u, 2), core, bit_x, bit_y, on_line(line), :]
        for _, device in peers:
            push(place, place, sent_sems.at[u, 2], gather_sems.at[u, 0], device)

    def spread_on(u, slot, place, device):
        push(place, place, sent_sems.at[u, 2], gather_sems.at[u, slot], device)

    def stage5(u):
        three = total_ref.at[pl.ds(2 * u, 2), core, bit_x, bit_y, pl.ds(0, 3 * piece), :]
        settled(three, gather_sems.at[u, 0])
        for j, device in ((0, to_y), (1, to_x)):
            spread_on(u, 1 + j, total_ref.at[2 * u + j, core, bit_x, bit_y], device)

    def stage6(u):
        for j, at, device in ((0, (bit_x,), to_x), (1, (slice(None), bit_y), to_y)):
            settled(total_ref.at[2 * u + j, core, bit_x, bit_y], gather_sems.at[u, 1 + j])
            spread_on(u, 3 + j, total_ref.at[(2 * u + j, core) + at], device)

    def stage7(u):
        for j in range(2):
            settled(total_ref.at[2 * u + j, core, bit_x], gather_sems.at[u, 3 + j])
        spread_on(u, 5, total_ref.at[pl.ds(2 * u, 2), core], other)

    outs = []

    def leave(source, target, at):
        outs.append(pltpu.make_async_copy(source, target, out_sems.at[at]))
        outs[-1].start()

    def stage8(u):
        settled(total_ref.at[pl.ds(2 * u, 2), core], gather_sems.at[u, 5])
        leave(total_ref.at[pl.ds(2 * u, 2)], total_hbm.at[pl.ds(2 * u, 2)], u)

    def all_sent(u):
        rows_sent = 2 * (4 + 2 + 1) * depth + 6 * piece
        by_lanes = glow_ref.at[pl.ds(0, rows_sent // 2), pl.ds(0, 2 * width)]
        settled(by_lanes, sent_sems.at[u, 0])
        settled(by_lanes, sent_sems.at[u, 2])
        settled(enc_t_ref.at[pl.ds(0, 24), pl.ds(0, width // 2)], sent_sems.at[u, 1])

    part_rows = small_ref.shape[0] // 2

    def small_send(slot, source, device):
        flights["s", slot] = send(source, small_take.at[slot], small_sems.at[slot], device)

    def small_step(stage):
        mine = pl.ds(pl.multiple_of(core * part_rows, part_rows), part_rows)
        if stage == 0:
            theirs = pl.ds(pl.multiple_of((1 - core) * part_rows, part_rows), part_rows)
            small_send(0, small_ref.at[theirs, :], other)
        elif stage == 1:
            flights["s", 0].wait_recv()
            small_now[0] = small_ref[mine, :] + small_take[0]
            small_send(1, small_now.at[0], to_x)
        elif stage == 2:
            flights["s", 1].wait_recv()
            small_now[1] = small_now[0] + small_take[1]
            small_send(2, small_now.at[1], to_y)
        elif stage == 3:
            flights["s", 2].wait_recv()
            small_now[2] = small_now[1] + small_take[2]
            for step, (_, device) in enumerate(peers):
                small_send(3 + step, small_now.at[2], device)
        elif stage == 4:
            for step in range(3):
                flights["s", 3 + step].wait_recv()
            value = (small_now[2] + small_take[3]) + (small_take[4] + small_take[5])
            for r in range(rounds):
                small_now[3 + r] = value
                small_send(6 + r, small_now.at[3 + r], far[r])
                flights["s", 6 + r].wait_recv()
                value = value + small_take[6 + r]
            small_total_ref[mine, :] = value
            place = small_total_ref.at[mine, :]
            flights["s", "last"] = send(place, place, small_sems.at[6 + rounds], other)
        elif stage == 5:
            flights["s", "last"].wait_recv()

    def own_lanes(b):
        return pl.ds(pl.multiple_of(b * frames + core * half, half), half)

    def far_lanes(b):
        return pl.ds(pl.multiple_of(b * frames + (1 - core) * half, half), half)

    def project(source, place):
        value = source[...].reshape(utts * half, enc_w_ref.shape[0])
        enc_proj = dot(value, enc_w_ref[...]) + enc_b_ref[...].astype(F32)[None, :]
        turned = jnp.transpose(enc_proj.astype(BF16).astype(F32))
        for b in range(utts):
            enc_t_ref[:, place(b)] = turned[:, b * half : (b + 1) * half]

    load_enc_w.wait()
    load_enc.wait()
    project(enc_own_ref, own_lanes)
    load_out_w.wait()
    out_wt_ref[pl.ds(0, vocab), :] = jnp.transpose(out_w_ref[...])
    bias_ref[pl.ds(0, vocab), :] = column_of(out_b_ref[...].astype(F32)[None, :])
    small_ref[...] = jnp.zeros(small_ref.shape, F32)
    blank_ref[...] = jnp.full(blank_ref.shape, NEGATIVE_FILL, F32)
    emit_ref[...] = jnp.full(emit_ref.shape, NEGATIVE_FILL, F32)
    low_ref[pl.ds(width, 16), :] = jnp.ones((16, low_ref.shape[1]), BF16)
    spread = jnp.where(iota((width, 4), 0) % 4 == iota((width, 4), 1), 1.0, 0.0).astype(BF16)
    same_group = iota((width, width), 0) // 4 == iota((width, width), 1) // 4
    group = width // 4
    widen = jnp.where(iota((group, width), 0) == iota((group, width), 1) // 4, 1.0, 0.0).astype(BF16)
    lane_out = iota((1, width), 1) % 4
    taps = []
    for tap in range(2):
        kernel_rows = []
        for i in range(4):
            spans = dot(conv_w_ref[tap, i], widen)
            row = jnp.zeros((1, width), F32)
            for o in range(4):
                row = jnp.where(lane_out == o, spans[o : o + 1], row)
            kernel_rows.append(row)
        kernel_rows = jnp.concatenate(kernel_rows, axis=0).astype(BF16)
        taps.append(jnp.where(same_group, dot(spread, kernel_rows), 0.0).astype(BF16))

    swap_labels.wait_recv()
    swap_starts.wait_recv()
    pieces = []
    for b in range(utts):
        own = labels_own_ref[pl.ds(first + b, 1), :].astype(F32)
        theirs = labels_far_ref[pl.ds(first + b, 1), :].astype(F32)
        pieces += [jnp.where(core == 0, own, theirs), jnp.where(core == 0, theirs, own)]
    label_row = jnp.concatenate(pieces, axis=1)
    for b in range(utts):
        for place, source in ((core, starts_own_ref), (1 - core, starts_far_ref)):
            starts_ref[pl.ds(b, 1), pl.ds(pl.multiple_of(place * half, half), half)] = source[
                pl.ds(first + b, 1), :
            ]
    within = iota((1, rows), 1) % positions
    token_row = jnp.where(within == 0, 0.0, pltpu.roll(label_row, 1, 1))
    label_col = column_of(label_row)
    token_col = column_of(token_row)
    vocab_lane = iota((rows, 128), 1).astype(F32)

    def one_hot(column):
        parts = [
            jnp.where(vocab_lane + float(at) == column, 1.0, 0.0).astype(BF16)
            for at in range(0, vocab, 128)
        ]
        return jnp.concatenate(parts, axis=1)

    row_within = iota((rows, width), 0) % positions
    load_table.wait()
    emb = dot(one_hot(token_col), table_ref[...])
    emb_prev = jnp.where(row_within == 0, 0.0, pltpu.roll(emb, 1, 0))
    emb_low = emb.astype(BF16)
    prev_low = emb_prev.astype(BF16)
    conv_out = dot(prev_low, taps[0]) + dot(emb_low, taps[1])
    conv_out = conv_out + conv_b_ref[...].astype(F32)[None, :]
    mean = jnp.mean(conv_out, axis=1, keepdims=True)
    centered = conv_out - mean
    rstd = lax.rsqrt(jnp.mean(centered * centered, axis=1, keepdims=True) + NORM_EPS)
    normed = centered * rstd
    gain = gain_ref[...].astype(F32)[None, :]
    scaled = normed * gain + shift_ref[...].astype(F32)[None, :]
    sigmoid = 1.0 / (1.0 + jnp.exp(-scaled))
    hidden = scaled * sigmoid
    hidden_low = hidden.astype(BF16)
    load_dec_w.wait()
    dec_proj = dot(hidden_low, dec_w_ref[...]) + dec_b_ref[...].astype(F32)[None, :]
    dec_t_ref[...] = jnp.transpose(dec_proj).astype(BF16)

    label_hot = one_hot(label_col)
    picks = pl.ds(vocab, rows)
    out_wt_ref[picks, :] = dot(label_hot, out_wt_ref[pl.ds(0, vocab), :]).astype(BF16)
    bias_ref[picks, :] = dot(label_hot, bias_ref[pl.ds(0, vocab), :].astype(BF16))
    wide_label = wide(label_col, frames // 128)
    swap_enc.wait_recv()
    project(enc_far_ref, far_lanes)

    block = 256

    def selector(b, k):
        begin = starts_ref[pl.ds(b, 1), :] + (k + b * positions)
        return iota((rows, frames), 0) == begin

    def chunk_lanes(c):
        return pl.ds(pl.multiple_of(c * frames, frames), frames)

    def utt_lanes(c):
        return pl.ds(pl.multiple_of((c // WINDOW) * frames, frames), frames)

    def activate(c):
        hot = jnp.where(selector(c // WINDOW, c % WINDOW), 1.0, 0.0).astype(BF16)
        act = jnp.tanh(enc_t_ref[:, utt_lanes(c)] + dot(dec_t_ref[...], hot))
        act_ref[c] = act
        low_ref[pl.ds(0, width), chunk_lanes(c)] = act.astype(BF16)

    def score(c, raw_ref):
        low = low_ref[pl.ds(0, width), chunk_lanes(c)]
        raw_ref[...] = dot(out_wt_ref[...], low) + wide(bias_ref[...], frames // 128)

    def normalise(c, raw_ref):
        b = c // WINDOW
        k = c % WINDOW
        top = jnp.max(raw_ref[pl.ds(0, vocab), :], axis=0, keepdims=True)
        total = jnp.zeros((1, frames), F32)
        for v in range(0, vocab, block):
            part = jnp.exp(raw_ref[pl.ds(v, block), :] - top)
            exp_ref[c, pl.ds(v, block), :] = part
            total = total + jnp.sum(part, axis=0, keepdims=True)
        log_norm = top + jnp.log(total)
        picked = selector(b, k)
        target = jnp.where(picked, raw_ref[pl.ds(vocab, rows), :], 0.0)
        target = jnp.sum(target, axis=0, keepdims=True) - log_norm
        live = starts_ref[pl.ds(b, 1), :] + k < lengths_ref[first + b]
        here = (pl.ds(k, 1), utt_lanes(c))
        blank_ref[here] = raw_ref[pl.ds(0, 1), :] - log_norm
        emit_ref[here] = jnp.where(live, target, NEGATIVE_FILL)
        inv_ref[here] = 1.0 / total
        wide_label_ref[here] = jnp.sum(jnp.where(picked, wide_label, 0.0), axis=0, keepdims=True)

    activate(0)
    activate(1)
    score(0, raw_a_ref)

    def forward(i, carry):
        c = 2 * i
        score(c + 1, raw_b_ref)
        normalise(c, raw_a_ref)
        activate(jnp.minimum(c + 2, chunks - 1))
        score(jnp.minimum(c + 2, chunks - 1), raw_a_ref)
        normalise(c + 1, raw_b_ref)
        activate(jnp.minimum(c + 3, chunks - 1))
        return carry

    lax.fori_loop(0, chunks // 2, forward, 0)

    starts_row = jnp.concatenate([starts_ref[b : b + 1, :] for b in range(utts)], axis=1)
    lane_row = iota((1, lanes), 1)
    moved = jnp.where(lane_row % frames == 0, 0, starts_row - pltpu.roll(starts_row, 1, 1))
    scale = jnp.zeros((1, lanes), F32)
    for b in range(utts):
        scale = jnp.where(lane_row // frames == b, -cot_ref[first + b] / frames, scale)
    leaving, blank_g, emit_g = lattice(blank_ref[...], emit_ref[...], moved, scale, frames)
    blank_g_ref[...] = blank_g
    emit_g_ref[...] = emit_g
    factor_ref[...] = -(blank_g + emit_g) * inv_ref[...]
    ends = iota((8, lanes), 1)
    for b in range(utts):
        last = (ends == (b + 1) * frames - 1) & (iota((8, lanes), 0) == WINDOW - 1)
        loss_ref[b] = -jnp.sum(jnp.where(last, leaving, 0.0)) / frames

    def logits_back(v):
        ids = iota((block, frames), 0) + v
        for c in range(chunks):
            b, k = c // WINDOW, c % WINDOW
            here = (slice(k, k + 1), slice(b * frames, (b + 1) * frames))
            blank_now, emit_now, factor = blank_g_ref[here], emit_g_ref[here], factor_ref[here]
            label_now = wide_label_ref[here].astype(jnp.int32)
            other_part = jnp.where(ids == 0, blank_now, 0.0) if v == 0 else 0.0
            grad = exp_ref[c, pl.ds(v, block), :] * factor + jnp.where(
                ids == label_now, emit_now, other_part
            )
            glow_ref[pl.ds(v, block), pl.ds(c * frames, frames)] = grad.astype(BF16)

    def weight_back(v):
        total = dot_nt(low_ref[...], glow_ref[pl.ds(v, block), :])
        grads_ref[v // width, :, :, :, :, pl.ds(v % width, block)] = total[:width].reshape(
            grads_ref.shape[1:5] + (block,)
        )
        small_ref[pl.ds(13 + v // width, 1), pl.ds(v % width, block)] = total[width : width + 1]

    logits_back(0)
    for v in range(0, vocab, block):
        weight_back(v)
        if v + block < vocab:
            logits_back(v + block)

    stage0(0)

    enc_sum_ref[...] = jnp.zeros(enc_sum_ref.shape, F32)
    dec_sum_ref[...] = jnp.zeros(dec_sum_ref.shape, F32)

    def pull(c, back_ref):
        back_ref[pl.ds(0, width), :] = dot(out_w_ref[...], glow_ref[:, chunk_lanes(c)])

    def settle(c, back_ref):
        act = act_ref[c]
        grad = back_ref[pl.ds(0, width), :] * (1.0 - act * act)
        enc_sum_ref[:, utt_lanes(c)] += grad
        hot = jnp.where(selector(c // WINDOW, c % WINDOW), 1.0, 0.0).astype(BF16)
        both = dot_nt(jnp.concatenate(halves(grad), axis=0), hot)
        dec_sum_ref[...] += both[:width] + both[width:]

    def backward(i, carry):
        c = 2 * i
        pull(c + 1, raw_b_ref)
        settle(c, raw_a_ref)
        pull(jnp.minimum(c + 2, chunks - 1), raw_a_ref)
        settle(c + 1, raw_b_ref)
        return carry

    pull(0, raw_a_ref)
    lax.fori_loop(0, 2, backward, 0)
    stage1(0)
    lax.fori_loop(2, chunks // 2, backward, 0)
    stage2(0)

    enc_b_grad = jnp.zeros((1, width), F32)
    enc_w_grad = jnp.zeros((enc_w_ref.shape[0], width), F32)
    for source, place, target in (
        (enc_far_ref, far_lanes, enc_g_send_ref),
        (enc_own_ref, own_lanes, enc_g_own_ref),
    ):
        enc_g = jnp.concatenate([enc_sum_ref[:, place(b)] for b in range(utts)], axis=1)
        enc_g = jnp.transpose(enc_g).astype(BF16)
        target[...] = enc_g.reshape(utts, half, width)
        value = source[...].reshape(utts * half, enc_w_ref.shape[0])
        enc_w_grad = enc_w_grad + dot(jnp.transpose(value), enc_g)
        enc_b_grad = enc_b_grad + jnp.sum(enc_g.astype(F32), axis=0, keepdims=True)
    grads_ref[2] = enc_w_grad.reshape(grads_ref.shape[1:])
    enc_copy = send(enc_g_send_ref, enc_g_far_hbm, enc_sems, other)
    leave(enc_g_own_ref, enc_g_own_hbm, UNITS)
    stage3(0)

    dec_g = jnp.transpose(dec_sum_ref[...]).astype(BF16)
    dec_b_grad = jnp.sum(dec_g.astype(F32), axis=0, keepdims=True)
    grads_ref[3] = dot(jnp.transpose(hidden).astype(BF16), dec_g).reshape(grads_ref.shape[1:])
    stage0(1)
    hidden_grad = dot_nt(dec_g, dec_w_ref[...])
    scaled_grad = hidden_grad * (sigmoid * (1.0 + scaled * (1.0 - sigmoid)))
    gain_grad = jnp.sum(scaled_grad * normed, axis=0, keepdims=True)
    shift_grad = jnp.sum(scaled_grad, axis=0, keepdims=True)
    normed_grad = scaled_grad * gain
    conv_grad = rstd * (
        normed_grad
        - jnp.mean(normed_grad, axis=1, keepdims=True)
        - normed * jnp.mean(normed_grad * normed, axis=1, keepdims=True)
    )
    high, rest = halves(conv_grad)
    prev_grad = dot_nt(high, taps[0]) + dot_nt(rest, taps[0])
    emb_grad = dot_nt(high, taps[1]) + dot_nt(rest, taps[1])
    emb_grad = emb_grad + jnp.where(
        row_within == positions - 1, 0.0, pltpu.roll(prev_grad, rows - 1, 0)
    )
    high, rest = halves(emb_grad)
    token_hot_t = jnp.where(
        iota((vocab, rows), 0) == token_row.astype(jnp.int32), 1.0, 0.0
    ).astype(BF16)
    for part in range(vocab // width):
        hot = token_hot_t[part * width : (part + 1) * width]
        table_grad = dot(hot, high) + dot(hot, rest)
        grads_ref[4 + part] = table_grad.reshape(grads_ref.shape[1:])
    stage0(2)
    stage1(1)
    stage4(0)

    conv_b_grad = jnp.sum(conv_grad, axis=0, keepdims=True)
    turned = halves(jnp.transpose(conv_grad))
    fold = jnp.where(iota((8, width), 1) % 4 == iota((8, width), 0), 1.0, 0.0).astype(BF16)
    for tap, source in enumerate((prev_low, emb_low)):
        outer = jnp.where(same_group, dot(turned[0], source) + dot(turned[1], source), 0.0)
        high, rest = halves(outer)
        folded = dot(fold, high) + dot(fold, rest)
        small_ref[pl.ds(4 * tap, 4), :] = folded[:4]
    for at, value in enumerate((conv_b_grad, gain_grad, shift_grad, dec_b_grad, enc_b_grad)):
        small_ref[pl.ds(8 + at, 1), :] = value

    small_step(0)
    stage1(2)
    stage2(1)
    stage5(0)
    small_step(1)
    stage2(2)
    stage3(1)
    stage6(0)
    small_step(2)
    stage3(2)
    stage4(1)
    stage7(0)
    small_step(3)
    stage4(2)
    stage5(1)
    stage8(0)
    small_step(4)
    stage5(2)
    stage6(1)
    small_step(5)
    stage6(2)
    stage7(1)
    stage7(2)
    stage8(1)
    stage8(2)
    for u in range(UNITS):
        all_sent(u)
    enc_copy.wait_recv()
    for copy in pending:
        copy.wait_send()
    for copy in outs:
        copy.wait()


def finish_kernel(
    share,
    loss_in_ref,
    small_ref,
    total_hbm,
    enc_g_own_hbm,
    enc_g_far_hbm,
    enc_w_hbm,
    loss_ref,
    enc_grad_hbm,
    table_hbm,
    conv_w_ref,
    conv_b_ref,
    gain_ref,
    shift_ref,
    dec_w_hbm,
    dec_b_ref,
    enc_w_grad_hbm,
    enc_b_ref,
    out_w_hbm,
    out_b_ref,
    enc_grad_ref,
    table_ref,
    dec_w_ref,
    enc_w_grad_ref,
    out_w_ref,
    total_ref,
    enc_g_own_ref,
    enc_g_far_ref,
    enc_w_ref,
    load_sems,
    sems,
):
    core = lax.axis_index("au")
    width = enc_w_ref.shape[1]
    loads = []
    for i in range(BLOCKS):
        loads.append((total_hbm.at[i], total_ref.at[i]))
    loads += [
        (enc_w_hbm, enc_w_ref),
        (enc_g_own_hbm, enc_g_own_ref),
        (enc_g_far_hbm, enc_g_far_ref),
    ]
    loads = [
        pltpu.make_async_copy(source, target, load_sems.at[at])
        for at, (source, target) in enumerate(loads)
    ]
    for load in loads:
        load.start()
    copies = []

    def leave(source, target):
        copies.append(pltpu.make_async_copy(source, target, sems.at[len(copies)]))
        copies[-1].start()

    for b in range(share):
        loss_ref[b] = loss_in_ref[b]
    for at, target in enumerate((conv_b_ref, gain_ref, shift_ref, dec_b_ref, enc_b_ref)):
        target[...] = small_ref[8 + at, :]
    out_b_ref[:width] = small_ref[13, :]
    out_b_ref[width:] = small_ref[14, :]
    group = width // 4
    high, rest = halves(small_ref[:8, :])
    last = (small_ref[:8, :] - high.astype(F32) - rest.astype(F32)).astype(BF16)
    for i in range(4):
        take = iota((width, group), 0) == 4 * iota((width, group), 1) + i
        take = jnp.where(take, 1.0, 0.0).astype(BF16)
        picked = dot(high, take) + dot(rest, take) + dot(last, take)
        for tap in range(2):
            conv_w_ref[tap, i] = picked[4 * tap : 4 * tap + 4]

    every = pl.ds(0, width)
    for i, target, home, where in (
        (0, out_w_ref, out_w_hbm, (every, pl.ds(0, width))),
        (1, out_w_ref, out_w_hbm, (every, pl.ds(width, width))),
        (2, enc_w_grad_ref, enc_w_grad_hbm, (every, every)),
        (3, dec_w_ref, dec_w_hbm, (every, every)),
        (4, table_ref, table_hbm, (pl.ds(0, width), every)),
        (5, table_ref, table_hbm, (pl.ds(width, width), every)),
    ):
        loads[i].wait()
        target[where] = total_ref[i].astype(F32).reshape(width, width)
        leave(target.at[where], home.at[where])
    loads[BLOCKS].wait()
    for at, source, place in (
        (BLOCKS + 1, enc_g_own_ref, core),
        (BLOCKS + 2, enc_g_far_ref, 1 - core),
    ):
        loads[at].wait()
        utts, half, _ = source.shape
        grad = dot_nt(source[...].reshape(utts * half, width), enc_w_ref[...])
        mine = pl.ds(place * share, share)
        enc_grad_ref[mine] = grad.reshape(utts, half, enc_w_ref.shape[0])
        leave(enc_grad_ref.at[mine], enc_grad_hbm.at[mine])
    for copy in copies:
        copy.wait()


def on_device(
    item_count,
    encoder_out,
    labels,
    lengths,
    starts,
    loss_cot,
    embed_table,
    conv_weight,
    conv_bias,
    norm_gain,
    norm_bias,
    dec_weight,
    dec_bias,
    enc_weight,
    enc_bias,
    out_weight,
    out_bias,
):
    utt_count, half, enc_dim = encoder_out.shape
    dec_dim = embed_table.shape[1]
    width, vocab = out_weight.shape
    share = utt_count // 2
    frames = 2 * half
    pairs = share * frames * WINDOW
    rows = share * 2 * labels.shape[1]
    lanes = share * frames
    chunks = share * WINDOW
    rounds = (item_count // 16).bit_length() - 1
    split = (2, 2, 2, width // 8, width)
    deep = max(rounds, 1)
    vmem = pl.BlockSpec(memory_space=pltpu.VMEM)
    smem = pl.BlockSpec(memory_space=pltpu.SMEM)
    anywhere = pl.BlockSpec(memory_space=pl.ANY)
    struct = jax.ShapeDtypeStruct
    mem = pltpu.VMEM
    dma = pltpu.SemaphoreType.DMA
    code = jnp.int16

    losses, enc_g_own, enc_g_far, small, totals = pl.pallas_call(
        functools.partial(main_kernel, share, rounds),
        out_shape=(
            struct((share,), F32),
            struct((share, half, width), BF16),
            struct((share, half, width), BF16),
            struct((16, width), F32),
            struct((BLOCKS,) + split, BF16),
        ),
        in_specs=[smem] * 2 + [vmem] * 9 + [anywhere] * 5,
        out_specs=(smem, anywhere, anywhere, vmem, anywhere),
        scratch_shapes=[
            mem(labels.shape, labels.dtype),
            mem(starts.shape, starts.dtype),
            mem((share, half, enc_dim), BF16),
            mem((share, half, enc_dim), BF16),
            mem(embed_table.shape, BF16),
            mem(dec_weight.shape, BF16),
            mem(enc_weight.shape, BF16),
            mem(out_weight.shape, BF16),
            mem((vocab + rows, width), BF16),
            mem((vocab + rows, 128), F32),
            mem((width, rows), BF16),
            mem((width, lanes), F32),
            mem((vocab + rows, frames), F32),
            mem((vocab + rows, frames), F32),
            mem((chunks, vocab, frames), F32),
            mem((chunks, width, frames), F32),
            mem((width + 16, pairs), BF16),
            mem((vocab, pairs), BF16),
        ]
        + [mem((8, lanes), F32)] * 7
        + [
            mem((width, lanes), F32),
            mem((width, rows), F32),
            mem((8, frames), jnp.int32),
            mem((BLOCKS,) + split, F32),
            mem((16, width), F32),
            mem((share, half, width), BF16),
            mem((share, half, width), BF16),
            mem((BLOCKS,) + split, BF16),
        ]
        + [
            mem((UNITS, 2) + split[1:], code),
            mem((UNITS, 2) + split[2:], code),
            mem((UNITS, 2) + split[3:], code),
        ]
        * 2
        + [
            mem((UNITS, 2, split[3], width), code),
            mem((UNITS, 3, 2, split[3] // 4, width), code),
            mem((UNITS, 6, 2, 1, width), F32),
            mem((UNITS, 6, 2, 1, width), F32),
            mem((3 + rounds, 8, width), F32),
            mem((6 + rounds, 8, width), F32),
            mem((deep, BLOCKS, split[3] // 4, width), F32),
            mem((deep, BLOCKS, split[3] // 4, width), F32),
            dma((5,)),
            dma((3, 2)),
            dma((UNITS, 6)),
            dma((UNITS, 6)),
            dma((UNITS, 6)),
            dma((UNITS, 3)),
            dma((7 + rounds, 2)),
            dma((deep, BLOCKS, 2)),
            dma((2,)),
            dma((UNITS + 1,)),
        ],
        compiler_params=pltpu.CompilerParams(
            collective_id=0, has_side_effects=True, vmem_limit_bytes=58 * MIB
        ),
        name="main",
    )(
        lengths,
        loss_cot,
        labels,
        starts,
        jnp.transpose(conv_weight, (0, 2, 3, 1)),
        conv_bias,
        norm_gain,
        norm_bias,
        dec_bias,
        enc_bias,
        out_bias,
        encoder_out,
        embed_table,
        dec_weight,
        enc_weight,
        out_weight,
    )

    vector = struct((width,), F32)
    square = struct((width, width), F32)
    outs = pl.pallas_call(
        functools.partial(finish_kernel, share),
        out_shape=(
            struct((share,), F32),
            struct(encoder_out.shape, F32),
            struct(embed_table.shape, F32),
            struct((2, 4, 4, dec_dim // 4), F32),
            vector,
            vector,
            vector,
            square,
            vector,
            square,
            vector,
            struct(out_weight.shape, F32),
            struct(out_bias.shape, F32),
        ),
        in_specs=[smem, vmem] + [anywhere] * 4,
        out_specs=(smem, anywhere, anywhere) + (vmem,) * 4 + (anywhere, vmem) * 3,
        scratch_shapes=[
            mem(encoder_out.shape, F32),
            mem(embed_table.shape, F32),
            mem((width, width), F32),
            mem((width, width), F32),
            mem(out_weight.shape, F32),
            mem((BLOCKS,) + split, BF16),
            mem((share, half, width), BF16),
            mem((share, half, width), BF16),
            mem(enc_weight.shape, BF16),
            dma((BLOCKS + 3,)),
            dma((BLOCKS + 2,)),
        ],
        compiler_params=pltpu.CompilerParams(vmem_limit_bytes=62 * MIB),
        name="finish",
    )(losses, small, totals, enc_g_own, enc_g_far, enc_weight)
    return outs[:3] + (jnp.transpose(outs[3], (0, 3, 1, 2)),) + outs[4:]


def solution(mesh):
    in_specs = (
        P("items", "au", None),
        P("items", "au"),
        P("items"),
        P("items", "au"),
        P("items"),
    ) + (P(),) * 11
    out_specs = (P(("items", "au")), P("items", "au", None)) + (P(),) * 11
    return jax.shard_map(
        functools.partial(on_device, mesh.shape["items"]),
        mesh=mesh,
        in_specs=in_specs,
        out_specs=out_specs,
        check_vma=False,
    )
```

time: 1610 us -> 79.4 us (0.05); the launches traced: 1590 us -> 79.1 us
  local copies, waits for them, and re-layouts: 967 us -> 0 us
  other arithmetic: 375 us -> 0 us
  waiting for transfers between devices: 110 us -> 0 us
  Pallas kernels: 0 us -> 78.3 us
  matrix products: 53.8 us -> 0 us
  blocking collectives: 43.3 us -> 0 us
    gather x1563 -> x0, local copies, waits for them, and re-layouts: 633 us -> none  [the longest x768 260 us: shift_window(): return jnp.take_along_axis(padded, picks, axis=1)]
    sub x257 -> x0, other arithmetic: 179 us -> none  [the longest x256 179 us: shift_back(): window_len - retreat[:, None]]
    squeeze x647 -> x0, local copies, waits for them, and re-layouts: 177 us -> none  [the longest x640 177 us: run_alpha(): lax.scan(advance_step, entry_vec, (blank_tm, emit_tm, advance_tm))]
    select_n x1048 -> x0, other arithmetic: 115 us -> none  [the longest x256 36.4 us: emit_backward(): jnp.logaddexp(blank_lp[:, column] + onward[:, column], emit_lp[:, column]...]
    psum x1 -> x0, waiting for transfers between devices: 110 us -> none  [on_device(): lax.psum((grad_set[0], grad_set[1], grad_set[2], grad_set[3], grad_set[4]...]
    pallas_call x0 -> x2, Pallas kernels: none -> 78.3 us  [the longest x1 72.7 us: on_device(): pl.pallas_call(functools.partial(main_kernel, share, rounds), out_shape=(...]
    dot_general x24 -> x0, matrix products: 53.8 us -> none  [the longest x4 13.7 us: joint_values(): jnp.dot(joint_low, out_weight, preferred_element_type=jnp.float32)]
    another operation x777 -> x0, local copies, waits for them, and re-layouts: 51.5 us -> none  [the longest x256 25.2 us: emit_forward(): return jnp.stack(columns, axis=1)]
where the time goes in v1:
time: 79.4 us; the launch traced here: 79.1 us
  Pallas kernels  78.3 us (99%)
  between operations  0.82 us (1%)
    pallas_call x1, Pallas kernels, on_device(): pl.pallas_call(functools.partial(main_kernel, share, rounds), out_shape=(...  72.7 us
    pallas_call x1, Pallas kernels, on_device(): pl.pallas_call(functools.partial(finish_kernel, share), out_shape=(struct...  5.64 us

profile of v1, /device:TPU:1, one launch (start us, length us, event | category | flops | bytes accessed | tf_op | source)
XLA Modules:
  0.0 79.1 jit_solution(10087801492368584647)
XLA Ops:
  0.7 72.7 %main.1 = (f32[2]{0:T(128)}, bf16[2,128,512]{2,1,0:T(8,128)(2,1)}, bf16[2,128,512]{2,1,0:T(8,128)(2,1)}, f32[16,512]{1,0:T(8,128)}, bf16[6,2,2,2,64,512]{5,4,3,2,1,0:T(8,128)(2,1)}) custom-call(s32[4]{0:T(128)} %lengths_ref.1, f32[4]{0:T(128)} %cot_ref.1, s32[4,32]{1,0:T(4,128)} %labels_own_ref.1, s32[4,128]{1,0:T(4,128)} %starts_own_ref.1, ...), custom_call_target="tpu_custom_call" | custom-call | tf_op jit(solution)/shard_map/main/pallas_call | solution.py:948
  73.3 5.6 %finish.1 = (f32[2]{0:T(128)}, f32[4,128,512]{2,1,0:T(8,128)}, f32[1024,512]{1,0:T(8,128)}, f32[2,4,4,128]{3,2,1,0:T(4,128)}, f32[512]{0:T(512)}, /*index=5*/f32...) custom-call(f32[2]{0:T(128)} %get-tuple-element.31.loss_in_ref, ...), custom_call_target="tpu_custom_call" | custom-call | tf_op jit(solution)/shard_map/finish/pallas_call | solution.py:1041

commit v2 on v1

--- a/solution.py
+++ b/solution.py
@@ -158,7 +158,7 @@
     loss_ref,
     enc_g_own_hbm,
     enc_g_far_hbm,
-    small_total_ref,
+    small_total_hbm,
     total_hbm,
     labels_far_ref,
     starts_far_ref,
@@ -193,6 +193,7 @@
     enc_g_send_ref,
     enc_g_own_ref,
     total_ref,
+    small_total_ref,
     send_core,
     send_one,
     send_two,
@@ -489,6 +490,7 @@
             flights["s", "last"] = send(place, place, small_sems.at[6 + rounds], other)
         elif stage == 5:
             flights["s", "last"].wait_recv()
+            leave(small_total_ref, small_total_hbm, UNITS + 1)
 
     def own_lanes(b):
         return pl.ds(pl.multiple_of(b * frames + core * half, half), half)
@@ -709,10 +711,8 @@
         return carry
 
     pull(0, raw_a_ref)
-    lax.fori_loop(0, 2, backward, 0)
+    lax.fori_loop(0, chunks // 2, backward, 0)
     stage1(0)
-    lax.fori_loop(2, chunks // 2, backward, 0)
-    stage2(0)
 
     enc_b_grad = jnp.zeros((1, width), F32)
     enc_w_grad = jnp.zeros((enc_w_ref.shape[0], width), F32)
@@ -729,7 +729,6 @@
     grads_ref[2] = enc_w_grad.reshape(grads_ref.shape[1:])
     enc_copy = send(enc_g_send_ref, enc_g_far_hbm, enc_sems, other)
     leave(enc_g_own_ref, enc_g_own_hbm, UNITS)
-    stage3(0)
 
     dec_g = jnp.transpose(dec_sum_ref[...]).astype(BF16)
     dec_b_grad = jnp.sum(dec_g.astype(F32), axis=0, keepdims=True)
@@ -760,8 +759,6 @@
         table_grad = dot(hot, high) + dot(hot, rest)
         grads_ref[4 + part] = table_grad.reshape(grads_ref.shape[1:])
     stage0(2)
-    stage1(1)
-    stage4(0)
 
     conv_b_grad = jnp.sum(conv_grad, axis=0, keepdims=True)
     turned = halves(jnp.transpose(conv_grad))
@@ -775,30 +772,20 @@
         small_ref[pl.ds(8 + at, 1), :] = value
 
     small_step(0)
-    stage1(2)
-    stage2(1)
-    stage5(0)
-    small_step(1)
-    stage2(2)
-    stage3(1)
-    stage6(0)
-    small_step(2)
-    stage3(2)
-    stage4(1)
-    stage7(0)
-    small_step(3)
-    stage4(2)
-    stage5(1)
-    stage8(0)
-    small_step(4)
-    stage5(2)
-    stage6(1)
-    small_step(5)
-    stage6(2)
-    stage7(1)
-    stage7(2)
-    stage8(1)
-    stage8(2)
+    order = (
+        ((2, 0), (1, 1), (3, 0), (1, 2)),
+        ((2, 1), (4, 0), (2, 2), (3, 1)),
+        ((3, 2), (5, 0), (4, 1)),
+        ((6, 0), (4, 2), (5, 1)),
+        ((7, 0), (5, 2), (6, 1)),
+        ((6, 2), (7, 1), (7, 2), (8, 1), (8, 0), (8, 2)),
+    )
+    stages = (stage0, stage1, stage2, stage3, stage4, stage5, stage6, stage7, stage8)
+    for at, steps in enumerate(order):
+        for stage, u in steps:
+            stages[stage](u)
+        if at < 5:
+            small_step(at + 1)
     for u in range(UNITS):
         all_sent(u)
     enc_copy.wait_recv()
@@ -811,7 +798,7 @@
 def finish_kernel(
     share,
     loss_in_ref,
-    small_ref,
+    small_hbm,
     total_hbm,
     enc_g_own_hbm,
     enc_g_far_hbm,
@@ -819,16 +806,16 @@
     loss_ref,
     enc_grad_hbm,
     table_hbm,
-    conv_w_ref,
-    conv_b_ref,
-    gain_ref,
-    shift_ref,
+    conv_w_hbm,
+    conv_b_hbm,
+    gain_hbm,
+    shift_hbm,
     dec_w_hbm,
-    dec_b_ref,
+    dec_b_hbm,
     enc_w_grad_hbm,
-    enc_b_ref,
+    enc_b_hbm,
     out_w_hbm,
-    out_b_ref,
+    out_b_hbm,
     enc_grad_ref,
     table_ref,
     dec_w_ref,
@@ -838,6 +825,10 @@
     enc_g_own_ref,
     enc_g_far_ref,
     enc_w_ref,
+    small_ref,
+    conv_w_ref,
+    vector_ref,
+    out_b_ref,
     load_sems,
     sems,
 ):
@@ -850,6 +841,7 @@
         (enc_w_hbm, enc_w_ref),
         (enc_g_own_hbm, enc_g_own_ref),
         (enc_g_far_hbm, enc_g_far_ref),
+        (small_hbm, small_ref),
     ]
     loads = [
         pltpu.make_async_copy(source, target, load_sems.at[at])
@@ -865,20 +857,6 @@
 
     for b in range(share):
         loss_ref[b] = loss_in_ref[b]
-    for at, target in enumerate((conv_b_ref, gain_ref, shift_ref, dec_b_ref, enc_b_ref)):
-        target[...] = small_ref[8 + at, :]
-    out_b_ref[:width] = small_ref[13, :]
-    out_b_ref[width:] = small_ref[14, :]
-    group = width // 4
-    high, rest = halves(small_ref[:8, :])
-    last = (small_ref[:8, :] - high.astype(F32) - rest.astype(F32)).astype(BF16)
-    for i in range(4):
-        take = iota((width, group), 0) == 4 * iota((width, group), 1) + i
-        take = jnp.where(take, 1.0, 0.0).astype(BF16)
-        picked = dot(high, take) + dot(rest, take) + dot(last, take)
-        for tap in range(2):
-            conv_w_ref[tap, i] = picked[4 * tap : 4 * tap + 4]
-
     every = pl.ds(0, width)
     for i, target, home, where in (
         (0, out_w_ref, out_w_hbm, (every, pl.ds(0, width))),
@@ -902,6 +880,24 @@
         mine = pl.ds(place * share, share)
         enc_grad_ref[mine] = grad.reshape(utts, half, enc_w_ref.shape[0])
         leave(enc_grad_ref.at[mine], enc_grad_hbm.at[mine])
+    loads[BLOCKS + 3].wait()
+    for at, home in enumerate((conv_b_hbm, gain_hbm, shift_hbm, dec_b_hbm, enc_b_hbm)):
+        vector_ref[at, :] = small_ref[8 + at, :]
+    out_b_ref[pl.ds(0, width)] = small_ref[13, :]
+    out_b_ref[pl.ds(width, width)] = small_ref[14, :]
+    for at, home in enumerate((conv_b_hbm, gain_hbm, shift_hbm, dec_b_hbm, enc_b_hbm)):
+        leave(vector_ref.at[at], home)
+    leave(out_b_ref, out_b_hbm)
+    group = width // 4
+    high, rest = halves(small_ref[:8, :])
+    last = (small_ref[:8, :] - high.astype(F32) - rest.astype(F32)).astype(BF16)
+    for i in range(4):
+        take = iota((width, group), 0) == 4 * iota((width, group), 1) + i
+        take = jnp.where(take, 1.0, 0.0).astype(BF16)
+        picked = dot(high, take) + dot(rest, take) + dot(last, take)
+        for tap in range(2):
+            conv_w_ref[tap, i] = picked[4 * tap : 4 * tap + 4]
+    leave(conv_w_ref, conv_w_hbm)
     for copy in copies:
         copy.wait()
 
@@ -955,7 +951,7 @@
             struct((BLOCKS,) + split, BF16),
         ),
         in_specs=[smem] * 2 + [vmem] * 9 + [anywhere] * 5,
-        out_specs=(smem, anywhere, anywhere, vmem, anywhere),
+        out_specs=(smem,) + (anywhere,) * 4,
         scratch_shapes=[
             mem(labels.shape, labels.dtype),
             mem(starts.shape, starts.dtype),
@@ -986,6 +982,7 @@
             mem((share, half, width), BF16),
             mem((share, half, width), BF16),
             mem((BLOCKS,) + split, BF16),
+            mem((16, width), F32),
         ]
         + [
             mem((UNITS, 2) + split[1:], code),
@@ -1011,7 +1008,7 @@
             dma((7 + rounds, 2)),
             dma((deep, BLOCKS, 2)),
             dma((2,)),
-            dma((UNITS + 1,)),
+            dma((UNITS + 2,)),
         ],
         compiler_params=pltpu.CompilerParams(
             collective_id=0, has_side_effects=True, vmem_limit_bytes=58 * MIB
@@ -1055,8 +1052,8 @@
             struct(out_weight.shape, F32),
             struct(out_bias.shape, F32),
         ),
-        in_specs=[smem, vmem] + [anywhere] * 4,
-        out_specs=(smem, anywhere, anywhere) + (vmem,) * 4 + (anywhere, vmem) * 3,
+        in_specs=[smem] + [anywhere] * 5,
+        out_specs=(smem,) + (anywhere,) * 12,
         scratch_shapes=[
             mem(encoder_out.shape, F32),
             mem(embed_table.shape, F32),
@@ -1067,8 +1064,12 @@
             mem((share, half, width), BF16),
             mem((share, half, width), BF16),
             mem(enc_weight.shape, BF16),
-            dma((BLOCKS + 3,)),
-            dma((BLOCKS + 2,)),
+            mem((16, width), F32),
+            mem((2, 4, 4, dec_dim // 4), F32),
+            mem((8, width), F32),
+            mem(out_bias.shape, F32),
+            dma((BLOCKS + 4,)),
+            dma((BLOCKS + 9,)),
         ],
         compiler_params=pltpu.CompilerParams(vmem_limit_bytes=62 * MIB),
         name="finish",

time: 79.4 us -> 78 us (0.982)
  Pallas kernels: 78.3 us -> 77 us
    pallas_call x1, Pallas kernels: 72.7 us -> 71.5 us  [on_device(): pl.pallas_call(functools.partial(main_kernel, share, rounds), out_shape=(...]
where the time goes in v2:
time: 78 us; the launch traced here: 77.8 us
  Pallas kernels  77 us (99%)
  between operations  0.82 us (1%)
    pallas_call x1, Pallas kernels, on_device(): pl.pallas_call(functools.partial(main_kernel, share, rounds), out_shape=(...  71.5 us
    pallas_call x1, Pallas kernels, on_device(): pl.pallas_call(functools.partial(finish_kernel, share), out_shape=(struct...  5.5 us

profile of v2, /device:TPU:1, one launch (start us, length us, event | category | flops | bytes accessed | tf_op | source)
XLA Modules:
  0.0 77.8 jit_solution(10602693338585582049)
XLA Ops:
  0.7 71.5 %main.1 = (f32[2]{0:T(128)}, bf16[2,128,512]{2,1,0:T(8,128)(2,1)}, bf16[2,128,512]{2,1,0:T(8,128)(2,1)}, f32[16,512]{1,0:T(8,128)}, bf16[6,2,2,2,64,512]{5,4,3,2,1,0:T(8,128)(2,1)}) custom-call(s32[4]{0:T(128)} %lengths_ref.1, f32[4]{0:T(128)} %cot_ref.1, s32[4,32]{1,0:T(4,128)} %labels_own_ref.1, s32[4,128]{1,0:T(4,128)} %starts_own_ref.1, ...), custom_call_target="tpu_custom_call" | custom-call | tf_op jit(solution)/shard_map/main/pallas_call | solution.py:944
  72.2 5.5 %finish.1 = (f32[2]{0:T(128)}, f32[4,128,512]{2,1,0:T(8,128)}, f32[1024,512]{1,0:T(8,128)}, f32[2,4,4,128]{3,2,1,0:T(4,128)}, f32[512]{0:T(512)}, /*index=5*/f32...) custom-call(f32[2]{0:T(128)} %get-tuple-element.31.loss_in_ref, ...), custom_call_target="tpu_custom_call" | custom-call | tf_op jit(solution)/shard_map/finish/pallas_call | solution.py:1038

commit v3 on v2

--- a/solution.py
+++ b/solution.py
@@ -784,8 +784,11 @@
     for at, steps in enumerate(order):
         for stage, u in steps:
             stages[stage](u)
-        if at < 5:
+        if at in (0, 1):
             small_step(at + 1)
+        elif at in (3, 4):
+            small_step(at)
+    small_step(5)
     for u in range(UNITS):
         all_sent(u)
     enc_copy.wait_recv()

time: 78 us -> 77.4 us (level)
  no operation moved by 1% of the time
where the time goes in v3:
time: 77.4 us; the launch traced here: 77.2 us
  Pallas kernels  76.3 us (99%)
  between operations  0.82 us (1%)
    pallas_call x1, Pallas kernels, on_device(): pl.pallas_call(functools.partial(main_kernel, share, rounds), out_shape=(...  70.8 us
    pallas_call x1, Pallas kernels, on_device(): pl.pallas_call(functools.partial(finish_kernel, share), out_shape=(struct...  5.5 us

profile of v3, /device:TPU:1, one launch (start us, length us, event | category | flops | bytes accessed | tf_op | source)
XLA Modules:
  0.0 77.2 jit_solution(14818880744176345803)
XLA Ops:
  0.7 70.8 %main.1 = (f32[2]{0:T(128)}, bf16[2,128,512]{2,1,0:T(8,128)(2,1)}, bf16[2,128,512]{2,1,0:T(8,128)(2,1)}, f32[16,512]{1,0:T(8,128)}, bf16[6,2,2,2,64,512]{5,4,3,2,1,0:T(8,128)(2,1)}) custom-call(s32[4]{0:T(128)} %lengths_ref.1, f32[4]{0:T(128)} %cot_ref.1, s32[4,32]{1,0:T(4,128)} %labels_own_ref.1, s32[4,128]{1,0:T(4,128)} %starts_own_ref.1, ...), custom_call_target="tpu_custom_call" | custom-call | tf_op jit(solution)/shard_map/main/pallas_call | solution.py:947
  71.5 5.5 %finish.1 = (f32[2]{0:T(128)}, f32[4,128,512]{2,1,0:T(8,128)}, f32[1024,512]{1,0:T(8,128)}, f32[2,4,4,128]{3,2,1,0:T(4,128)}, f32[512]{0:T(512)}, /*index=5*/f32...) custom-call(f32[2]{0:T(128)} %get-tuple-element.31.loss_in_ref, ...), custom_call_target="tpu_custom_call" | custom-call | tf_op jit(solution)/shard_map/finish/pallas_call | solution.py:1041
